TPU v7x, 512 devices: a whole 4x4x16 slice. The times are simulated.
512 devices in a mesh: tok: 8 (over y, core), voc: 64 (over z, x).
Axes of the slice: x: 4, y: 4, z: 16, core: 2. Of those that a mesh axis runs over, the one named last changes fastest.
Arguments:
- teacher_batch: bfloat16 [160, 5120], P('tok'), may hold values from -210 to 210
- student_batch: bfloat16 [160, 3584], P('tok'), may hold values from -140 to 140
- positions: int32 [128], P('tok'), may hold values from 0 to 19
- teacher_head: bfloat16 [5120, 81920], P('tok', 'voc'), may hold values from -0.078125 to 0.078125
- student_head: bfloat16 [3584, 81920], P('tok', 'voc'), may hold values from -0.09375 to 0.09375
Outputs:
- head_grad: bfloat16 [3584, 81920], P('tok', 'voc')
- token_loss: float32 [128], P('tok')
All inputs are finite; a program needn't handle non-finite values.
Results may differ from a plain program's by a relative error of at most 0.005.
Values may be sent and summed in bfloat16 or wider, within the bound.
A program may use at most 64 MiB of HBM per device.

v0:
```python
import math

import jax
import jax.numpy as jnp
from jax import lax
from jax.sharding import PartitionSpec as P


def row_statistics(teacher_logits, student_logits):
    top_teacher, top_student = lax.pmax(
        (jnp.max(teacher_logits, axis=1), jnp.max(student_logits, axis=1)), "voc"
    )
    shifted = jnp.exp(teacher_logits - top_teacher[:, None])
    sum_teacher, moment, cross_sum, sum_student = lax.psum(
        (
            jnp.sum(shifted, axis=1),
            jnp.sum(shifted * teacher_logits, axis=1),
            jnp.sum(shifted * student_logits, axis=1),
            jnp.sum(jnp.exp(student_logits - top_student[:, None]), axis=1),
        ),
        "voc",
    )
    teacher_lse = top_teacher + jnp.log(sum_teacher)
    student_lse = top_student + jnp.log(sum_student)
    entropy = teacher_lse - moment / sum_teacher
    cross_mean = cross_sum / sum_teacher
    return (teacher_lse, student_lse, entropy, cross_mean)


def on_device(teacher_batch, student_batch, positions, teacher_head, student_head):
    tok_rows = positions.shape[0]
    vocab_shard = teacher_head.shape[1]
    vocab_size = vocab_shard * lax.axis_size("voc")
    log_vocab = math.log(vocab_size)
    teacher_rows = jnp.take(teacher_batch, positions, axis=0)
    student_rows = jnp.take(student_batch, positions, axis=0)
    teacher_cols, student_cols = (
        lax.all_to_all(teacher_rows, "tok", split_axis=1, concat_axis=0, tiled=True),
        lax.all_to_all(student_rows, "tok", split_axis=1, concat_axis=0, tiled=True),
    )
    teacher_part = jnp.dot(teacher_cols, teacher_head, preferred_element_type=jnp.float32)
    student_part = jnp.dot(student_cols, student_head, preferred_element_type=jnp.float32)
    logits = lax.psum_scatter(
        jnp.concatenate([teacher_part, student_part], axis=1),
        "tok",
        scatter_dimension=0,
        tiled=True,
    )
    teacher_logits = logits[:, :vocab_shard]
    student_logits = logits[:, vocab_shard:]
    teacher_lse, student_lse, entropy, cross_mean = row_statistics(teacher_logits, student_logits)
    weight = jnp.exp(-2.0 * entropy / log_vocab)
    token_loss = weight * (student_lse - cross_mean - entropy)
    teacher_prob = jnp.exp(teacher_logits - teacher_lse[:, None])
    student_prob = jnp.exp(student_logits - student_lse[:, None])
    logit_grad = (vocab_size / tok_rows * weight[:, None] * (student_prob - teacher_prob)).astype(
        jnp.bfloat16
    )
    head_total = lax.dot_general(
        student_cols,
        lax.all_gather(logit_grad, "tok", axis=0, tiled=True),
        (((0,), (0,)), ((), ())),
        preferred_element_type=jnp.float32,
    )
    return (head_total.astype(jnp.bfloat16), token_loss)


def solution(mesh):
    in_specs = (P("tok", None), P("tok", None), P("tok"), P("tok", "voc"), P("tok", "voc"))
    out_specs = (P("tok", "voc"), P("tok"))
    return jax.shard_map(
        on_device, mesh=mesh, in_specs=in_specs, out_specs=out_specs, check_vma=False
    )
```

profile of v0, /device:TPU:1, one launch (start us, length us, event | category | flops | bytes accessed | tf_op | source)
XLA Modules:
  0.0 384.3 jit_solution(13413994397292665722)
XLA Ops:
  7.2 0.0 copy-start
  7.2 0.0 copy-start.1
  7.2 0.8 compare_and_fusion
  8.0 0.7 compare_select_fusion
  8.7 1.7 gather_fusion
  10.3 0.2 gather.13
  10.5 0.7 copy_select_fusion
  11.2 10.1 %all-to-all-start = ((bf16[16,8,448]{2,0,1:T(8,128)(2,1)}), bf16[16,8,448]{2,0,1:T(8,128)(2,1)S(1)}, u32[]{:S(2)}, u32[]{:S(2)}) async-start(bf16[16,8,448]{2,0,1:T(8,128)(2,1)} %copy_select_fusion), calls=%async_computation | async-start | bytes 262144 | tf_op jit(solution)/shard_map/all_to_all | solution.py:39
  21.4 0.0 copy-done.1
  21.4 0.6 gather_fusion.1
  22.0 0.8 bitcast_select_fusion
  22.8 3.9 %all-to-all-done = bf16[16,8,448]{2,0,1:T(8,128)(2,1)S(1)} async-done(((bf16[16,8,448]{2,0,1:T(8,128)(2,1)}), bf16[16,8,448]{2,0,1:T(8,128)(2,1)S(1)}, u32[]{:S(2)}, u32[]{:S(2)}) %all-to-all-start) | async-done | bytes 114720 | tf_op jit(solution)/shard_map/all_to_all | solution.py:39
  26.7 4.1 %all-to-all-start.1 = ((bf16[16,8,640]{2,0,1:T(8,128)(2,1)}), bf16[16,8,640]{2,0,1:T(8,128)(2,1)S(1)}, u32[]{:S(2)}, u32[]{:S(2)}) async-start(bf16[16,8,640]{2,0,1:T(8,128)(2,1)} %bitcast_select_fusion), calls=%async_computation.1 | async-start | bytes 327680 | tf_op jit(solution)/shard_map/all_to_all | solution.py:38
  30.8 0.0 reduce-scatter.2.cloned.1.call-start
  30.8 1.6 fusion.3
  32.4 4.0 %all-to-all-done.1 = bf16[16,8,640]{2,0,1:T(8,128)(2,1)S(1)} async-done(((bf16[16,8,640]{2,0,1:T(8,128)(2,1)}), bf16[16,8,640]{2,0,1:T(8,128)(2,1)S(1)}, u32[]{:S(2)}, u32[]{:S(2)}) %all-to-all-start.1) | async-done | bytes 163872 | tf_op jit(solution)/shard_map/all_to_all | solution.py:38
  36.4 0.0 copy-done
  36.4 0.4 fusion.2
  36.9 1.2 pad_maximum_fusion
  38.1 0.0 reduce-scatter.2.cloned.1.call-update
  38.1 36.9 %reduce-scatter.2.cloned.1.call-done = f32[16,2560]{1,0:T(8,128)} async-done(((f32[128,2560]{1,0:T(8,128)}), f32[16,2560]{1,0:T(8,128)}) %reduce-scatter.2.cloned.1.call-update) | async-done | bytes 163856 | tf_op jit(solution)/shard_map/reduce_scatter | solution.py:43
  75.0 1.0 slice_reduce_fusion
  76.0 115.4 %all-reduce.1 = (f32[16]{0:T(128)S(1)}, f32[16]{0:T(128)S(1)}) all-reduce(f32[16]{0:T(128)S(1)} %get-tuple-element.7, f32[16]{0:T(128)S(1)} %get-tuple-element.6), channel_id=1, replica_groups=mesh['tok'=8,'voc'=64] {'voc'}, use_global_device_ids=true, to_apply=%region_2.3 | all-reduce | flops 32 | bytes 256 | tf_op jit(solution)/shard_map/pmax | solution.py:10
  191.4 1.2 multiply_reduce_fusion
  192.6 110.1 %all-reduce = (f32[16]{0:T(128)S(1)}, f32[16]{0:T(128)S(1)}, f32[16]{0:T(128)S(1)}, f32[16]{0:T(128)S(1)}) all-reduce(f32[16]{0:T(128)S(1)} %get-tuple-element.3, f32[16]{0:T(128)S(1)} %get-tuple-element.5, f32[16]{0:T(128)S(1)} %get-tuple-element.4, f32[16]{0:T(128)S(1)} %get-tuple-element.2), channel_id=1, replica_groups=mesh['tok'=8,'voc'=64] {'voc'}, use_global_device_ids=true, to_apply=%region_4.5 | all-reduce | flops 64 | bytes 512 | tf_op jit(solution)/shard_map/psum | solution.py:14
  302.7 0.5 subtract_multiply_fusion
  303.2 1.0 multiply_convert_fusion
  304.3 71.7 %all_gather.3 = bf16[128,1280]{1,0:T(8,128)(2,1)S(1)} all-gather(bf16[16,1280]{1,0:T(8,128)(2,1)S(1)} %multiply_convert_fusion), channel_id=1, replica_groups=mesh['tok'=8,'voc'=64] {'tok'}, dimensions={0}, use_global_device_ids=true | all-gather | bytes 368640 | tf_op jit(solution)/shard_map/all_gather | solution.py:61
  376.0 1.5 convolution_convert_fusion
  (2 shorter events, 0.0 us)
Async XLA Ops:
  7.2 29.3 %copy-start = (bf16[640,1280]{1,0:T(8,128)(2,1)S(1)}, bf16[640,1280]{1,0:T(8,128)(2,1)}, u32[]{:S(2)}) copy-start(bf16[640,1280]{1,0:T(8,128)(2,1)} %param.8) | copy-start | bytes 4915204
  7.2 14.2 %copy-start.1 = (bf16[20,5120]{1,0:T(8,128)(2,1)S(1)}, bf16[20,5120]{1,0:T(8,128)(2,1)}, u32[]{:S(2)}) copy-start(bf16[20,5120]{1,0:T(8,128)(2,1)} %param.5) | copy-start | bytes 614404
  11.2 15.4 %all-to-all-start = ((bf16[16,8,448]{2,0,1:T(8,128)(2,1)}), bf16[16,8,448]{2,0,1:T(8,128)(2,1)S(1)}, u32[]{:S(2)}, u32[]{:S(2)}) async-start(bf16[16,8,448]{2,0,1:T(8,128)(2,1)} %copy_select_fusion), calls=%async_computation | async-start | bytes 262144 | tf_op jit(solution)/shard_map/all_to_all | solution.py:39
  26.7 9.8 %all-to-all-start.1 = ((bf16[16,8,640]{2,0,1:T(8,128)(2,1)}), bf16[16,8,640]{2,0,1:T(8,128)(2,1)S(1)}, u32[]{:S(2)}, u32[]{:S(2)}) async-start(bf16[16,8,640]{2,0,1:T(8,128)(2,1)} %bitcast_select_fusion), calls=%async_computation.1 | async-start | bytes 327680 | tf_op jit(solution)/shard_map/all_to_all | solution.py:38
  30.8 44.1 %reduce-scatter.2.cloned.1.call-start = ((), (), s32[]{:S(2)}) async-start(), calls=%async_computation.3 | async-start | bytes 1474560 | tf_op jit(solution)/shard_map/reduce_scatter | solution.py:43
Sparse Core Ops, SparseCore 0:
  38.2 36.7 reduce-scatter.1
where the time goes:
time: 385 us; the launch traced here: 384 us
  blocking collectives  297 us (77%)
  waiting for transfers between devices  44.8 us (12%)
  starting transfers between devices  14.3 us (4%)
  between operations  14.1 us (4%)
  other arithmetic  7.93 us (2%)
    pmax x1, blocking collectives, row_statistics(): lax.pmax((jnp.max(teacher_logits, axis=1), jnp.max(student_logits, axis=1...  115 us
    psum x1, blocking collectives, row_statistics(): lax.psum((jnp.sum(shifted, axis=1), jnp.sum(shifted * teacher_logits, axi...  110 us
    all_gather x1, blocking collectives, on_device(): lax.all_gather(logit_grad, 'tok', axis=0, tiled=True)  71.7 us
    reduce_scatter x1, waiting for transfers between devices, on_device(): lax.psum_scatter(jnp.concatenate([teacher_part, student_part], axis=1), '...  36.9 us
    all_to_all x1, starting transfers between devices, on_device(): lax.all_to_all(student_rows, 'tok', split_axis=1, concat_axis=0, tiled=True)  10.1 us
  transfers between devices with their start and end apart: 3, of which 3 were waited for; matrix products, arithmetic and copies ran while one was open for 1% of the time, Pallas kernels for 0%

commit v1 on v0

v1 whole, which is shorter than its diff:
```python
import functools
import math

import jax
import jax.numpy as jnp
from jax import lax
from jax.experimental import pallas as pl
from jax.experimental.pallas import tpu as pltpu
from jax.sharding import PartitionSpec as P

MESH = pl.DeviceIdType.MESH
F32 = jnp.float32
BF16 = jnp.bfloat16
NY, NC, NX, NZ = 4, 2, 4, 16
TOK = 16
ROWS = NY * NC * TOK
STEP = 256


def remote(src, dst, send, recv, target):
    return pltpu.make_async_remote_copy(
        src_ref=src, dst_ref=dst, send_sem=send, recv_sem=recv, device_id=target, device_id_type=MESH
    )


def combine(rows):
    tops = pltpu.roll(rows, 64, axis=1)
    top = jnp.max(tops, axis=0, keepdims=True)
    total = jnp.sum(rows * jnp.exp(tops - top), axis=0, keepdims=True)
    lane = lax.broadcasted_iota(jnp.int32, (1, 128), 1)
    return jnp.where(lane < 64, total, pltpu.roll(jnp.broadcast_to(top, (8, 128)), 64, axis=1)[:1])


def exchange_kernel(
    vocab, width_t, width_s, shard,
    tb_hbm, sb_hbm, pos_ref, th_hbm, sh_hbm,
    grad_ref, cols_ref, loss_ref,
    tb, sb, th, sh, picked, states, part, sib, chip, rs, xbuf, zbuf,
    load_sem, st_send, st_recv, sib_send, sib_recv, rs_send, rs_recv, x_send, x_recv, z_send, z_recv, g_send, g_recv,
):
    chunks = shard // STEP
    tok, voc = lax.axis_index("tok"), lax.axis_index("voc")
    y, c = tok // NC, tok % NC
    z, x = voc // NX, voc % NX

    def tok_peer(k, r):
        return (((y + k) % NY) * NC + (c + r) % NC, voc)

    def x_peer(d):
        return (tok, z * NX + (x + d) % NX)

    def z_peer(d):
        return (tok, ((z + d) % NZ) * NX + x)

    tok_peers = [(k, r) for k in (2, 1, 3, 0) for r in range(NC) if (k, r) != (0, 0)]

    loads = [
        pltpu.make_async_copy(src, dst, load_sem.at[i])
        for i, (src, dst) in enumerate(((tb_hbm, tb), (sb_hbm, sb), (th_hbm, th), (sh_hbm, sh)))
    ]
    for load in loads:
        load.start()

    barrier = pltpu.get_barrier_semaphore()
    peers = [tok_peer(k, r) for k, r in tok_peers]
    peers += [x_peer(d) for d in range(1, NX)] + [z_peer(d) for d in range(1, NZ)]
    for peer in peers:
        pl.semaphore_signal(barrier, inc=1, device_id=peer, device_id_type=MESH)

    sub = lax.broadcasted_iota(jnp.int32, (TOK, TOK), 0)
    lane = lax.broadcasted_iota(jnp.int32, (TOK, TOK), 1)
    spread = jnp.where(sub == lane, jnp.broadcast_to(pos_ref[...], (TOK, TOK)), 0).astype(F32)
    column = jnp.sum(spread, axis=1, keepdims=True).astype(jnp.int32)
    n_pos = tb.shape[0]
    onehot = (lax.broadcasted_iota(jnp.int32, (TOK, n_pos), 1) == column).astype(BF16)
    loads[0].wait()
    loads[1].wait()
    pl.semaphore_wait(barrier, len(peers))

    state_copies = {}
    for k in (2, 1, 3, 0):
        yk = (y + k) % NY
        t_off = pl.multiple_of(yk * (NC * width_t), 128)
        s_off = pl.multiple_of(yk * (NC * width_s), 128)
        t_rows = jnp.dot(onehot, tb[:, pl.ds(t_off, NC * width_t)], preferred_element_type=F32)
        s_rows = jnp.dot(onehot, sb[:, pl.ds(s_off, NC * width_s)], preferred_element_type=F32)
        for h in range(NC):
            picked[k, h, :, :width_t] = t_rows[:, h * width_t : (h + 1) * width_t].astype(BF16)
            picked[k, h, :, width_t : width_t + width_s] = s_rows[:, h * width_s : (h + 1) * width_s].astype(BF16)
        for r in range(NC):
            if (k, r) == (0, 0):
                continue
            slot = r * NY + (NY - k) % NY
            copy = remote(
                picked.at[k, (c + r) % NC],
                states.at[slot * TOK : (slot + 1) * TOK],
                st_send.at[r * NY + k],
                st_recv.at[slot],
                tok_peer(k, r),
            )
            copy.start()
            state_copies[r * NY + k] = copy
    states[:TOK] = picked[0, c]
    for copy in state_copies.values():
        copy.wait_recv()
    loads[2].wait()
    loads[3].wait()

    sib_copies, rs_copies = [], []

    def pass_on(j):
        sib_copies[j].wait_recv()
        chip[j] = part[j, : ROWS // 2] + sib[j]
        for k in (2, 1, 3):
            copy = remote(
                chip.at[j, k * TOK : (k + 1) * TOK],
                rs.at[j, k - 1],
                rs_send.at[j, k - 1],
                rs_recv.at[j, k - 1],
                tok_peer(k, 0),
            )
            copy.start()
            rs_copies.append(copy)

    for j in range(chunks):
        cols = slice(j * STEP, (j + 1) * STEP)
        part[j, :, :STEP] = jnp.dot(states[:, :width_t], th[:, cols], preferred_element_type=F32)
        part[j, :, STEP:] = jnp.dot(
            states[:, width_t : width_t + width_s], sh[:, cols], preferred_element_type=F32
        )
        copy = remote(part.at[j, ROWS // 2 :], sib.at[j], sib_send.at[j], sib_recv.at[j], tok_peer(0, 1))
        copy.start()
        sib_copies.append(copy)
        if j >= 1:
            pass_on(j - 1)
    pass_on(chunks - 1)

    cols_ref[...] = jnp.transpose(states[:, width_t : width_t + width_s].astype(F32)).astype(BF16)

    for copy in rs_copies:
        copy.wait_recv()
    t_parts, s_parts = [], []
    for j in range(chunks):
        total = (chip[j, :TOK] + rs[j, 0]) + (rs[j, 1] + rs[j, 2])
        t_parts.append(total[:, :STEP])
        s_parts.append(total[:, STEP:])
    t_log = jnp.concatenate(t_parts, axis=1)
    s_log = jnp.concatenate(s_parts, axis=1)

    top_t = jnp.max(t_log, axis=1, keepdims=True)
    top_s = jnp.max(s_log, axis=1, keepdims=True)
    shifted = jnp.exp(t_log - top_t)
    columns = [
        jnp.sum(shifted, axis=1, keepdims=True),
        jnp.sum(shifted * t_log, axis=1, keepdims=True),
        jnp.sum(shifted * s_log, axis=1, keepdims=True),
        jnp.sum(jnp.exp(s_log - top_s), axis=1, keepdims=True),
        top_t, top_t, top_t, top_s,
    ]
    sub = lax.broadcasted_iota(jnp.int32, (TOK, 128), 0)
    lane = lax.broadcasted_iota(jnp.int32, (TOK, 128), 1)
    packed = jnp.zeros((TOK, 128), F32)
    for k, value in enumerate(columns):
        packed = jnp.where(lane == sub + k * TOK, value, packed)
    row = jnp.sum(packed, axis=0, keepdims=True)

    def all_rows(buf, n, row, peer, send, recv):
        buf[n - 1 : n] = row
        copies = [
            remote(buf.at[n - 1 : n], buf.at[d - 1 : d], send.at[d - 1], recv.at[d - 1], peer(d)) for d in range(1, n)
        ]
        for copy in copies:
            copy.start()
        for copy in copies:
            copy.wait_recv()
        return copies, combine(buf[...])

    x_copies, row = all_rows(xbuf, NX, row, x_peer, x_send, x_recv)
    z_copies, row = all_rows(zbuf, NZ, row, z_peer, z_send, z_recv)

    spread = jnp.broadcast_to(row, (TOK, 128))
    sum_t, moment, cross, sum_s, top_t, top_s = (
        jnp.sum(jnp.where(lane == sub + k * TOK, spread, 0.0), axis=1, keepdims=True) for k in (0, 1, 2, 3, 4, 7)
    )
    t_lse = top_t + jnp.log(sum_t)
    s_lse = top_s + jnp.log(sum_s)
    entropy = t_lse - moment / sum_t
    weight = jnp.exp(-2.0 * entropy / math.log(vocab))
    loss = weight * (s_lse - cross / sum_t - entropy)
    grad = (vocab / TOK * weight) * (jnp.exp(s_log - s_lse) - jnp.exp(t_log - t_lse))
    grad_ref[:TOK] = grad.astype(BF16)
    g_copies = []
    for k, r in tok_peers:
        slot = r * NY + (NY - k) % NY
        copy = remote(
            grad_ref.at[:TOK],
            grad_ref.at[slot * TOK : (slot + 1) * TOK],
            g_send.at[r * NY + k],
            g_recv.at[slot],
            tok_peer(k, r),
        )
        copy.start()
        g_copies.append(copy)
    loss_ref[...] = jnp.sum(jnp.where(lane == sub, loss, 0.0), axis=0, keepdims=True)

    for copy in [*state_copies.values(), *sib_copies, *rs_copies, *x_copies, *z_copies]:
        copy.wait_send()
    for copy in g_copies:
        copy.wait()


def final_kernel(cols_ref, grad_ref, loss_in, head_ref, loss_ref):
    head_ref[...] = jnp.dot(cols_ref[...], grad_ref[...], preferred_element_type=F32).astype(BF16)
    loss_ref[...] = loss_in[:, :TOK]


def on_device(teacher_batch, student_batch, positions, teacher_head, student_head):
    width_t, shard = teacher_head.shape
    width_s = student_head.shape[0]
    vocab = shard * NX * NZ
    chunks = shard // STEP
    wide = 128 * pl.cdiv(width_t + width_s, 128)
    any_spec = pl.BlockSpec(memory_space=pl.ANY)
    vmem = pl.BlockSpec(memory_space=pltpu.VMEM)
    dma = pltpu.SemaphoreType.DMA
    grad, cols, loss = pl.pallas_call(
        functools.partial(exchange_kernel, vocab, width_t, width_s, shard),
        out_shape=(
            jax.ShapeDtypeStruct((ROWS, shard), BF16),
            jax.ShapeDtypeStruct((width_s, ROWS), BF16),
            jax.ShapeDtypeStruct((1, 128), F32),
        ),
        in_specs=[any_spec, any_spec, vmem, any_spec, any_spec],
        out_specs=(vmem, vmem, vmem),
        scratch_shapes=[
            pltpu.VMEM(teacher_batch.shape, BF16),
            pltpu.VMEM(student_batch.shape, BF16),
            pltpu.VMEM(teacher_head.shape, BF16),
            pltpu.VMEM(student_head.shape, BF16),
            pltpu.VMEM((NY, NC, TOK, wide), BF16),
            pltpu.VMEM((ROWS, wide), BF16),
            pltpu.VMEM((chunks, ROWS, 2 * STEP), F32),
            pltpu.VMEM((chunks, ROWS // 2, 2 * STEP), F32),
            pltpu.VMEM((chunks, ROWS // 2, 2 * STEP), F32),
            pltpu.VMEM((chunks, NY - 1, TOK, 2 * STEP), F32),
            pltpu.VMEM((NX, 128), F32),
            pltpu.VMEM((NZ, 128), F32),
            dma((4,)),
            dma((8,)), dma((8,)),
            dma((chunks,)), dma((chunks,)),
            dma((chunks, 3)), dma((chunks, 3)),
            dma((NX - 1,)), dma((NX - 1,)),
            dma((NZ - 1,)), dma((NZ - 1,)),
            dma((8,)), dma((8,)),
        ],
        compiler_params=pltpu.CompilerParams(
            collective_id=0, has_side_effects=True
        ),
    )(teacher_batch, student_batch, positions.reshape(1, TOK), teacher_head, student_head)
    head_grad, loss = pl.pallas_call(
        final_kernel,
        out_shape=(
            jax.ShapeDtypeStruct((width_s, shard), BF16),
            jax.ShapeDtypeStruct((1, TOK), F32),
        ),
        in_specs=[vmem] * 3,
        out_specs=(vmem, vmem),
    )(cols, grad, loss)
    return head_grad, loss.reshape(TOK)


def solution(mesh):
    in_specs = (P("tok", None), P("tok", None), P("tok"), P("tok", "voc"), P("tok", "voc"))
    out_specs = (P("tok", "voc"), P("tok"))
    return jax.shard_map(
        on_device, mesh=mesh, in_specs=in_specs, out_specs=out_specs, check_vma=False
    )
```

time: 385 us -> 54 us (0.14)
  blocking collectives: 297 us -> 0 us
  Pallas kernels: 0 us -> 53.2 us
  waiting for transfers between devices: 44.8 us -> 0 us
  starting transfers between devices: 14.3 us -> 0 us
  between operations: 14.1 us -> 0.64 us
  other arithmetic: 7.93 us -> 0 us
    pmax x1 -> x0, blocking collectives: 115 us -> none  [row_statistics(): lax.pmax((jnp.max(teacher_logits, axis=1), jnp.max(student_logits, axis=1...]
    psum x1 -> x0, blocking collectives: 110 us -> none  [row_statistics(): lax.psum((jnp.sum(shifted, axis=1), jnp.sum(shifted * teacher_logits, axi...]
    all_gather x1 -> x0, blocking collectives: 71.7 us -> none  [on_device(): lax.all_gather(logit_grad, 'tok', axis=0, tiled=True)]
    pallas_call x0 -> x2, Pallas kernels: none -> 53.2 us  [the longest x1 50.7 us: on_device(): pl.pallas_call(functools.partial(exchange_kernel, vocab, width_t, width_s...]
    reduce_scatter x1 -> x0, waiting for transfers between devices: 36.9 us -> none  [on_device(): lax.psum_scatter(jnp.concatenate([teacher_part, student_part], axis=1), '...]
    all_to_all x2 -> x0, starting transfers between devices: 14.3 us -> none  [the longest x1 10.1 us: on_device(): lax.all_to_all(student_rows, 'tok', split_axis=1, concat_axis=0, tiled=True)]
    all_to_all x2 -> x0, waiting for transfers between devices: 7.88 us -> none  [the longest x1 3.99 us: on_device(): lax.all_to_all(teacher_rows, 'tok', split_axis=1, concat_axis=0, tiled=True)]
  transfers between devices with their start and end apart: 3 -> 0, of which waited for: 3 -> 0; matrix products, arithmetic and copies ran while one was open for 1% -> 0% of each run, Pallas kernels for 0% -> 0%
where the time goes in v1:
time: 54 us; the launch traced here: 53.8 us
  Pallas kernels  53.2 us (99%)
  between operations  0.64 us (1%)
    pallas_call x1, Pallas kernels, on_device(): pl.pallas_call(functools.partial(exchange_kernel, vocab, width_t, width_s...  50.7 us
    pallas_call x1, Pallas kernels, on_device(): pl.pallas_call(final_kernel, out_shape=(jax.ShapeDtypeStruct((width_s, sh...  2.45 us

profile of v1, /device:TPU:1, one launch (start us, length us, event | category | flops | bytes accessed | tf_op | source)
XLA Modules:
  0.0 53.8 jit_solution(9063737390420913639)
XLA Ops:
  0.6 50.7 %shard_map.68 = (bf16[128,1280]{1,0:T(8,128)(2,1)}, bf16[448,128]{1,0:T(8,128)(2,1)}, f32[1,128]{1,0:T(1,128)}) custom-call(bf16[20,5120]{1,0:T(8,128)(2,1)} %tb_hbm.1, bf16[20,3584]{1,0:T(8,128)(2,1)} %sb_hbm.1, s32[1,16]{1,0:T(1,128)} %bitcast.2, bf16[640,1280]{1,0:T(8,128)(2,1)} %th_hbm.1, bf16[448,1280]{1,0:T(8,128)(2,1)} %sh_hbm.1), custom_call_target="tpu_custom_call" | custom-call | tf_op jit(solution)/shard_map/pallas_call | solution.py:226
  51.4 2.5 %shard_map.69 = (bf16[448,1280]{1,0:T(8,128)(2,1)}, f32[1,16]{1,0:T(1,128)}) custom-call(bf16[448,128]{1,0:T(8,128)(2,1)} %get-tuple-element.7.cols_ref, bf16[128,1280]{1,0:T(8,128)(2,1)} %get-tuple-element.8.grad_ref, f32[1,128]{1,0:T(1,128)} %get-tuple-element.9.loss_in), custom_call_target="tpu_custom_call" | custom-call | tf_op jit(solution)/shard_map/pallas_call | solution.py:260

commit v2 on v1

v2 whole, which is shorter than its diff:
```python
import functools
import math

import jax
import jax.numpy as jnp
from jax import lax
from jax.experimental import pallas as pl
from jax.experimental.pallas import tpu as pltpu
from jax.sharding import PartitionSpec as P

MESH = pl.DeviceIdType.MESH
F32 = jnp.float32
BF16 = jnp.bfloat16
NY, NC, NX, NZ = 4, 2, 4, 16
TOK = 16
PAIR = NC * TOK
ROWS = NY * PAIR
PLACE = {0: 0, 1: 1, 3: 2, 2: 3}
BACK = {0: 0, 1: 3, 2: 2, 3: 1}


def slot_of(k, r):
    return PLACE[k] * NC + r


def remote(src, dst, send, recv, target):
    return pltpu.make_async_remote_copy(
        src_ref=src, dst_ref=dst, send_sem=send, recv_sem=recv, device_id=target, device_id_type=MESH
    )


def lanes(values, start):
    return pltpu.roll(values, (128 - start) % 128, axis=values.ndim - 1) if start else values


def combine(rows):
    tops = pltpu.roll(rows, 64, axis=2)
    top = jnp.max(tops, axis=0)
    total = jnp.sum(rows * jnp.exp(tops - top[None]), axis=0)
    lane = lax.broadcasted_iota(jnp.int32, total.shape, 1)
    return jnp.where(lane < 64, total, pltpu.roll(top, 64, axis=1))


def exchange_kernel(
    vocab, width_t, width_s, shard,
    tb_hbm, sb_hbm, pos_ref, th_hbm, sh_hbm,
    grad_ref, cols_ref, loss_ref,
    tb, sb, th, sh, picked, states, part, sib, chip, opp, merged, ring, logits, shifted, tops, zbuf, pbuf,
    load_sem, st_send, st_recv, sib_send, sib_recv, opp_send, opp_recv, ring_send, ring_recv,
    lg_send, lg_recv, z_sem, p_sem, go, far,
):
    tok, voc = lax.axis_index("tok"), lax.axis_index("voc")
    y, c = tok // NC, tok % NC
    z, x = voc // NX, voc % NX

    def device(k, r, dx=0, dz=0):
        return (((y + k) % NY) * NC + (c + r) % NC, ((z + dz) % NZ) * NX + (x + dx) % NX)

    def core(k, which, dx=0, dz=0):
        return (((y + k) % NY) * NC + which, ((z + dz) % NZ) * NX + (x + dx) % NX)

    loads = [
        pltpu.make_async_copy(src, dst, load_sem.at[i])
        for i, (src, dst) in enumerate(((tb_hbm, tb), (sb_hbm, sb), (th_hbm, th), (sh_hbm, sh)))
    ]
    loads[0].start()
    loads[1].start()

    barrier = pltpu.get_barrier_semaphore()
    for k in (2, 1, 3):
        pl.semaphore_signal(barrier, inc=1, device_id=core(k, 0), device_id_type=MESH)

    @pl.when(c == 1)
    def _():
        pl.semaphore_signal(barrier, inc=1, device_id=core(0, 0), device_id_type=MESH)

    loads[2].start()
    loads[3].start()

    sub = lax.broadcasted_iota(jnp.int32, (TOK, TOK), 0)
    lane = lax.broadcasted_iota(jnp.int32, (TOK, TOK), 1)
    spread = jnp.where(sub == lane, jnp.broadcast_to(pos_ref[...], (TOK, TOK)), 0).astype(F32)
    column = jnp.sum(spread, axis=1, keepdims=True).astype(jnp.int32)
    onehot = (lax.broadcasted_iota(jnp.int32, (TOK, tb.shape[0]), 1) == column).astype(BF16)
    loads[0].wait()
    loads[1].wait()

    def pick(k):
        yk = (y + k) % NY
        t_off = pl.multiple_of(yk * (NC * width_t), 128)
        s_off = pl.multiple_of(yk * (NC * width_s), 128)
        t_rows = jnp.dot(onehot, tb[:, pl.ds(t_off, NC * width_t)], preferred_element_type=F32)
        s_rows = jnp.dot(onehot, sb[:, pl.ds(s_off, NC * width_s)], preferred_element_type=F32)
        for h in range(NC):
            picked[k, h, :, :width_t] = t_rows[:, h * width_t : (h + 1) * width_t].astype(BF16)
            picked[k, h, :, width_t : width_t + width_s] = s_rows[:, h * width_s : (h + 1) * width_s].astype(BF16)

    pick(2)

    @pl.when(c == 0)
    def _():
        pl.semaphore_wait(barrier, NY * NC - 1)
        pl.semaphore_signal(go, inc=1, device_id=core(0, 1), device_id_type=MESH)

    @pl.when(c == 1)
    def _():
        pl.semaphore_wait(go, 1)

    sent = []
    arrived = {}

    def start(copy):
        copy.start()
        sent.append(copy)
        return copy

    for k in (2, 1, 3, 0):
        if k != 2:
            pick(k)
        for r in range(NC):
            if (k, r) != (0, 0):
                slot = slot_of(BACK[k], r)
                arrived[BACK[k], r] = start(remote(
                    picked.at[k, (c + r) % NC],
                    states.at[slot * TOK : (slot + 1) * TOK],
                    st_send.at[slot], st_recv.at[slot], device(k, r),
                ))
    states[:TOK] = picked[0, c]

    for dz in range(1, NZ):
        pl.semaphore_signal(barrier, inc=1, device_id=core(0, 1, 0, dz), device_id_type=MESH)
    for dx in range(1, NX):
        for k in range(NY):
            pl.semaphore_signal(barrier, inc=1, device_id=core(k, 1, dx, 0), device_id_type=MESH)

    def multiply(ks):
        first = min(PLACE[k] for k in ks) * PAIR
        rows = slice(first, first + len(ks) * PAIR)
        for m in range(2):
            if m == 0:
                part[m, rows] = jnp.dot(states[rows, :width_t], th[...], preferred_element_type=F32)
            else:
                part[m, rows] = jnp.dot(
                    states[rows, width_t : width_t + width_s], sh[...], preferred_element_type=F32
                )
            for k in ks:
                at = PLACE[k]
                sib_copies[m, k] = start(remote(
                    part.at[m, at * PAIR + TOK : (at + 1) * PAIR],
                    sib.at[m, at], sib_send.at[m, at], sib_recv.at[m, at], device(0, 1),
                ))

    def add_cores(m, k):
        sib_copies[m, k].wait_recv()
        at = PLACE[k]
        chip[m, at] = part[m, at * PAIR : at * PAIR + TOK] + sib[m, at]

    sib_copies = {}
    loads[2].wait()
    loads[3].wait()
    arrived[0, 1].wait_recv()
    multiply((0,))
    for r in range(NC):
        arrived[2, r].wait_recv()
    multiply((2,))
    for k in (1, 3):
        for r in range(NC):
            arrived[k, r].wait_recv()
    multiply((1, 3))

    opp_copies = []
    for m, k in ((0, 1), (1, 3)):
        add_cores(m, 2)
        opp_copies.append(start(remote(
            chip.at[m, PLACE[2]], opp.at[m], opp_send.at[m], opp_recv.at[m], device(k, 0)
        )))
    ring_copies = {}
    for m, k in ((1, 1), (0, 3)):
        add_cores(m, k)
        ring_copies[m, k] = start(remote(
            chip.at[m, PLACE[k]], ring.at[m, k // 2], ring_send.at[m, k // 2], ring_recv.at[m, k // 2], device(k, 0)
        ))
    for m, k in ((0, 1), (1, 3)):
        add_cores(m, k)
    for m, k in ((0, 1), (1, 3)):
        opp_copies[m].wait_recv()
        merged[m] = chip[m, PLACE[k]] + opp[m]
        ring_copies[m, k] = start(remote(
            merged.at[m], ring.at[m, k // 2], ring_send.at[m, k // 2], ring_recv.at[m, k // 2], device(k, 0)
        ))
    add_cores(0, 0)
    add_cores(1, 0)
    cols_ref[...] = jnp.transpose(states[:, width_t : width_t + width_s].astype(F32)).astype(BF16)

    for copy in ring_copies.values():
        copy.wait_recv()
    t_log = chip[0, 0] + (ring[0, 0] + ring[0, 1])
    s_log = chip[1, 0] + (ring[1, 0] + ring[1, 1])
    logits[0, 0] = t_log
    logits[0, 1] = s_log

    top_t = jnp.max(t_log, axis=1, keepdims=True)
    top_s = jnp.max(s_log, axis=1, keepdims=True)
    exp_t = jnp.exp(t_log - top_t)
    exp_s = jnp.exp(s_log - top_s)
    columns = [
        jnp.sum(exp_t, axis=1, keepdims=True),
        jnp.sum(exp_t * t_log, axis=1, keepdims=True),
        jnp.sum(exp_t * s_log, axis=1, keepdims=True),
        jnp.sum(exp_s, axis=1, keepdims=True),
        top_t, top_t, top_t, top_s,
    ]
    sub = lax.broadcasted_iota(jnp.int32, (TOK, 128), 0)
    lane = lax.broadcasted_iota(jnp.int32, (TOK, 128), 1)
    packed = jnp.zeros((TOK, 128), F32)
    for k, value in enumerate(columns):
        packed = jnp.where(lane == sub + k * TOK, value, packed)
    zbuf[0:1] = jnp.sum(packed, axis=0, keepdims=True)

    @pl.when(c == 1)
    def _():
        pl.semaphore_wait(barrier, NC * ((NZ - 1) + (NX - 1) * NY))
        pl.semaphore_signal(far, inc=1, device_id=core(0, 0), device_id_type=MESH)

    @pl.when(c == 0)
    def _():
        pl.semaphore_wait(far, 1)

    for dz in sorted(range(1, NZ), key=lambda d: -min(d, NZ - d)):
        remote(zbuf.at[0:1], zbuf.at[NZ - dz : NZ - dz + 1], z_sem.at[0], z_sem.at[1], device(0, 0, 0, dz)).start()

    lg_copies = {}

    def to_other_core(k):
        mine = slot_of(k, 0)
        lg_copies[k, 1] = start(remote(
            logits.at[mine], logits.at[slot_of(k, 1)], lg_send.at[slot_of(k, 1)], lg_recv.at[slot_of(k, 1)], device(0, 1)
        ))

    for k in (1, 3, 2):
        slot = slot_of(BACK[k], 0)
        lg_copies[BACK[k], 0] = start(remote(
            logits.at[0], logits.at[slot], lg_send.at[slot], lg_recv.at[slot], device(k, 0)
        ))
    to_other_core(0)

    def exponents(slot, values):
        for m in range(2):
            top = jnp.max(values[m], axis=1, keepdims=True)
            shifted[slot, m] = jnp.exp(values[m] - top)
            tops[slot, m] = jnp.broadcast_to(top, (TOK, 128))

    def arrive(k, r):
        lg_copies[k, r].wait_recv()
        if r == 0:
            to_other_core(k)
        slot = slot_of(k, r)
        exponents(slot, (logits[slot, 0], logits[slot, 1]))

    shifted[0, 0] = exp_t
    shifted[0, 1] = exp_s
    tops[0, 0] = jnp.broadcast_to(top_t, (TOK, 128))
    tops[0, 1] = jnp.broadcast_to(top_s, (TOK, 128))
    arrive(0, 1)
    arrive(1, 0)
    arrive(3, 0)

    pltpu.make_async_copy(zbuf.at[1:NZ], zbuf.at[1:NZ], z_sem.at[1]).wait()
    pbuf[0:1] = combine(zbuf[...].reshape(NZ, 1, 128))
    plane = [(dx, k, r) for dx in (2, 1, 3, 0) for k in (2, 1, 3, 0) for r in range(NC) if (dx, k, r) != (0, 0, 0)]
    for dx, k, r in plane:
        row = BACK[dx] * NY * NC + slot_of(BACK[k], r)
        remote(pbuf.at[0:1], pbuf.at[row : row + 1], p_sem.at[0], p_sem.at[1], device(k, r, dx)).start()

    arrive(1, 1)
    arrive(3, 1)
    arrive(2, 0)
    arrive(2, 1)

    everyone = pbuf.at[1 : NX * NY * NC]
    pltpu.make_async_copy(everyone, everyone, p_sem.at[1]).wait()
    rows = combine(pbuf[...].reshape(NX, NY * NC, 128))

    sum_t = rows
    t_lse = lanes(rows, 4 * TOK) + jnp.log(sum_t)
    s_lse = lanes(rows, 7 * TOK) + jnp.log(lanes(rows, 3 * TOK))
    entropy = t_lse - lanes(rows, TOK) / sum_t
    weight = jnp.exp(-2.0 * entropy / math.log(vocab))
    loss_ref[...] = (weight * (s_lse - lanes(rows, 2 * TOK) / sum_t - entropy))[0:1]

    lane = lax.broadcasted_iota(jnp.int32, (NY * NC, TOK, 128), 2)
    sub = lax.broadcasted_iota(jnp.int32, (NY * NC, TOK, 128), 1)

    def column_of(values):
        spread = jnp.broadcast_to(values[:, None, :], (NY * NC, TOK, 128))
        return jnp.sum(jnp.where(lane == sub, spread, 0.0), axis=2, keepdims=True)

    scale = column_of(vocab / TOK * weight)
    scale_t = scale * jnp.exp(tops[:, 0] - column_of(t_lse))
    scale_s = scale * jnp.exp(tops[:, 1] - column_of(s_lse))
    for slot in range(NY * NC):
        grad = scale_s[slot, :, 0:1] * shifted[slot, 1] - scale_t[slot, :, 0:1] * shifted[slot, 0]
        grad_ref[slot * TOK : (slot + 1) * TOK] = grad.astype(BF16)

    for copy in sent:
        copy.wait_send()
    pltpu.make_async_copy(zbuf.at[1:NZ], zbuf.at[1:NZ], z_sem.at[0]).wait()
    pltpu.make_async_copy(everyone, everyone, p_sem.at[0]).wait()


def final_kernel(pieces, cols_ref, grad_ref, loss_in, head_hbm, loss_ref, head, sem):
    rows = head.shape[0] // pieces
    copies = []
    for i in range(pieces):
        at = slice(i * rows, (i + 1) * rows)
        head[at] = jnp.dot(cols_ref[at], grad_ref[...], preferred_element_type=F32).astype(BF16)
        copy = pltpu.make_async_copy(head.at[at], head_hbm.at[at], sem.at[i])
        copy.start()
        copies.append(copy)
    loss_ref[...] = loss_in[:, :TOK]
    for copy in copies:
        copy.wait()


def on_device(teacher_batch, student_batch, positions, teacher_head, student_head):
    width_t, shard = teacher_head.shape
    width_s = student_head.shape[0]
    vocab = shard * NX * NZ
    wide = 128 * pl.cdiv(width_t + width_s, 128)
    groups = NY * NC
    any_spec = pl.BlockSpec(memory_space=pl.ANY)
    vmem = pl.BlockSpec(memory_space=pltpu.VMEM)
    dma = pltpu.SemaphoreType.DMA
    grad, cols, loss = pl.pallas_call(
        functools.partial(exchange_kernel, vocab, width_t, width_s, shard),
        out_shape=(
            jax.ShapeDtypeStruct((ROWS, shard), BF16),
            jax.ShapeDtypeStruct((width_s, ROWS), BF16),
            jax.ShapeDtypeStruct((1, 128), F32),
        ),
        in_specs=[any_spec, any_spec, vmem, any_spec, any_spec],
        out_specs=(vmem, vmem, vmem),
        scratch_shapes=[
            pltpu.VMEM(teacher_batch.shape, BF16),
            pltpu.VMEM(student_batch.shape, BF16),
            pltpu.VMEM(teacher_head.shape, BF16),
            pltpu.VMEM(student_head.shape, BF16),
            pltpu.VMEM((NY, NC, TOK, wide), BF16),
            pltpu.VMEM((ROWS, wide), BF16),
            pltpu.VMEM((2, ROWS, shard), F32),
            pltpu.VMEM((2, NY, TOK, shard), F32),
            pltpu.VMEM((2, NY, TOK, shard), F32),
            pltpu.VMEM((2, TOK, shard), F32),
            pltpu.VMEM((2, TOK, shard), F32),
            pltpu.VMEM((2, 2, TOK, shard), F32),
            pltpu.VMEM((groups, 2, TOK, shard), F32),
            pltpu.VMEM((groups, 2, TOK, shard), F32),
            pltpu.VMEM((groups, 2, TOK, 128), F32),
            pltpu.VMEM((NZ, 128), F32),
            pltpu.VMEM((NX * groups, 128), F32),
            dma((4,)),
            dma((groups,)), dma((groups,)),
            dma((2, NY)), dma((2, NY)),
            dma((2,)), dma((2,)),
            dma((2, 2)), dma((2, 2)),
            dma((groups,)), dma((groups,)),
            dma((2,)), dma((2,)),
            pltpu.SemaphoreType.REGULAR,
            pltpu.SemaphoreType.REGULAR,
        ],
        compiler_params=pltpu.CompilerParams(collective_id=0, has_side_effects=True),
    )(teacher_batch, student_batch, positions.reshape(1, TOK), teacher_head, student_head)
    pieces = 4
    head_grad, loss = pl.pallas_call(
        functools.partial(final_kernel, pieces),
        out_shape=(
            jax.ShapeDtypeStruct((width_s, shard), BF16),
            jax.ShapeDtypeStruct((1, TOK), F32),
        ),
        in_specs=[vmem] * 3,
        out_specs=(any_spec, vmem),
        scratch_shapes=[pltpu.VMEM((width_s, shard), BF16), dma((pieces,))],
    )(cols, grad, loss)
    return head_grad, loss.reshape(TOK)


def solution(mesh):
    in_specs = (P("tok", None), P("tok", None), P("tok"), P("tok", "voc"), P("tok", "voc"))
    out_specs = (P("tok", "voc"), P("tok"))
    return jax.shard_map(
        on_device, mesh=mesh, in_specs=in_specs, out_specs=out_specs, check_vma=False
    )
```

time: 54 us -> 48.1 us (0.89)
  Pallas kernels: 53.2 us -> 47.3 us
    pallas_call x1, Pallas kernels: 50.7 us -> 44.5 us  [on_device(): pl.pallas_call(functools.partial(exchange_kernel, vocab, width_t, width_s...]
where the time goes in v2:
time: 48.1 us; the launch traced here: 47.9 us
  Pallas kernels  47.3 us (98%)
  between operations  0.64 us (1%)
    pallas_call x1, Pallas kernels, on_device(): pl.pallas_call(functools.partial(exchange_kernel, vocab, width_t, width_s...  44.5 us
    pallas_call x1, Pallas kernels, on_device(): pl.pallas_call(functools.partial(final_kernel, pieces), out_shape=(jax.Sh...  2.78 us

profile of v2, /device:TPU:1, one launch (start us, length us, event | category | flops | bytes accessed | tf_op | source)
XLA Modules:
  0.0 47.9 jit_solution(6001740711113834511)
XLA Ops:
  0.6 44.5 %shard_map.68 = (bf16[128,1280]{1,0:T(8,128)(2,1)}, bf16[448,128]{1,0:T(8,128)(2,1)}, f32[1,128]{1,0:T(1,128)}) custom-call(bf16[20,5120]{1,0:T(8,128)(2,1)} %tb_hbm.1, bf16[20,3584]{1,0:T(8,128)(2,1)} %sb_hbm.1, s32[1,16]{1,0:T(1,128)} %bitcast.2, bf16[640,1280]{1,0:T(8,128)(2,1)} %th_hbm.1, bf16[448,1280]{1,0:T(8,128)(2,1)} %sh_hbm.1), custom_call_target="tpu_custom_call" | custom-call | tf_op jit(solution)/shard_map/pallas_call | solution.py:334
  45.1 2.8 %shard_map.69 = (bf16[448,1280]{1,0:T(8,128)(2,1)}, f32[1,16]{1,0:T(1,128)}) custom-call(bf16[448,128]{1,0:T(8,128)(2,1)} %get-tuple-element.7.cols_ref, bf16[128,1280]{1,0:T(8,128)(2,1)} %get-tuple-element.8.grad_ref, f32[1,128]{1,0:T(1,128)} %get-tuple-element.9.loss_in), custom_call_target="tpu_custom_call" | custom-call | tf_op jit(solution)/shard_map/pallas_call | solution.py:374

commit v3 on v2

--- a/solution.py
+++ b/solution.py
@@ -13,6 +13,7 @@
 BF16 = jnp.bfloat16
 NY, NC, NX, NZ = 4, 2, 4, 16
 TOK = 16
+CLERK = 4
 PAIR = NC * TOK
 ROWS = NY * PAIR
 PLACE = {0: 0, 1: 1, 3: 2, 2: 3}
@@ -43,9 +44,9 @@
 
 def exchange_kernel(
     vocab, width_t, width_s, shard,
-    tb_hbm, sb_hbm, pos_ref, th_hbm, sh_hbm,
+    tb_hbm, sb_hbm, pos_hbm, th_hbm, sh_hbm,
     grad_ref, cols_ref, loss_ref,
-    tb, sb, th, sh, picked, states, part, sib, chip, opp, merged, ring, logits, shifted, tops, zbuf, pbuf,
+    tb, sb, pos, th, sh, picked, states, part, sib, chip, opp, merged, ring, logits, shifted, tops, zbuf, pbuf,
     load_sem, st_send, st_recv, sib_send, sib_recv, opp_send, opp_recv, ring_send, ring_recv,
     lg_send, lg_recv, z_sem, p_sem, go, far,
 ):
@@ -56,34 +57,31 @@
     def device(k, r, dx=0, dz=0):
         return (((y + k) % NY) * NC + (c + r) % NC, ((z + dz) % NZ) * NX + (x + dx) % NX)
 
-    def core(k, which, dx=0, dz=0):
-        return (((y + k) % NY) * NC + which, ((z + dz) % NZ) * NX + (x + dx) % NX)
-
     loads = [
         pltpu.make_async_copy(src, dst, load_sem.at[i])
-        for i, (src, dst) in enumerate(((tb_hbm, tb), (sb_hbm, sb), (th_hbm, th), (sh_hbm, sh)))
+        for i, (src, dst) in enumerate(((pos_hbm, pos), (tb_hbm, tb), (sb_hbm, sb), (th_hbm, th), (sh_hbm, sh)))
     ]
-    loads[0].start()
-    loads[1].start()
+    for load in loads[:3]:
+        load.start()
 
     barrier = pltpu.get_barrier_semaphore()
-    for k in (2, 1, 3):
-        pl.semaphore_signal(barrier, inc=1, device_id=core(k, 0), device_id_type=MESH)
-
-    @pl.when(c == 1)
-    def _():
-        pl.semaphore_signal(barrier, inc=1, device_id=core(0, 0), device_id_type=MESH)
-
-    loads[2].start()
-    loads[3].start()
-
+    clerk = tok == CLERK
+    for k, r in ((2, 0), (2, 1), (1, 0), (1, 1), (3, 0), (3, 1), (0, 1)):
+        @pl.when(device(k, r)[0] != CLERK)
+        def _():
+            pl.semaphore_signal(barrier, inc=1, device_id=device(k, r), device_id_type=MESH)
+
+    for load in loads[3:]:
+        load.start()
+
+    loads[0].wait()
     sub = lax.broadcasted_iota(jnp.int32, (TOK, TOK), 0)
     lane = lax.broadcasted_iota(jnp.int32, (TOK, TOK), 1)
-    spread = jnp.where(sub == lane, jnp.broadcast_to(pos_ref[...], (TOK, TOK)), 0).astype(F32)
+    spread = jnp.where(sub == lane, jnp.broadcast_to(pos[...], (TOK, TOK)), 0).astype(F32)
     column = jnp.sum(spread, axis=1, keepdims=True).astype(jnp.int32)
     onehot = (lax.broadcasted_iota(jnp.int32, (TOK, tb.shape[0]), 1) == column).astype(BF16)
-    loads[0].wait()
     loads[1].wait()
+    loads[2].wait()
 
     def pick(k):
         yk = (y + k) % NY
@@ -97,12 +95,15 @@
 
     pick(2)
 
-    @pl.when(c == 0)
+    @pl.when(jnp.logical_not(clerk))
     def _():
         pl.semaphore_wait(barrier, NY * NC - 1)
-        pl.semaphore_signal(go, inc=1, device_id=core(0, 1), device_id_type=MESH)
-
-    @pl.when(c == 1)
+
+    @pl.when(device(0, 1)[0] == CLERK)
+    def _():
+        pl.semaphore_signal(go, inc=1, device_id=device(0, 1), device_id_type=MESH)
+
+    @pl.when(clerk)
     def _():
         pl.semaphore_wait(go, 1)
 
@@ -127,11 +128,9 @@
                 ))
     states[:TOK] = picked[0, c]
 
-    for dz in range(1, NZ):
-        pl.semaphore_signal(barrier, inc=1, device_id=core(0, 1, 0, dz), device_id_type=MESH)
-    for dx in range(1, NX):
-        for k in range(NY):
-            pl.semaphore_signal(barrier, inc=1, device_id=core(k, 1, dx, 0), device_id_type=MESH)
+    for dx, dz in [(0, dz) for dz in range(1, NZ)] + [(dx, 0) for dx in range(1, NX)]:
+        there = (CLERK, device(0, 0, dx, dz)[1])
+        pl.semaphore_signal(barrier, inc=1, device_id=there, device_id_type=MESH)
 
     def multiply(ks):
         first = min(PLACE[k] for k in ks) * PAIR
@@ -156,8 +155,8 @@
         chip[m, at] = part[m, at * PAIR : at * PAIR + TOK] + sib[m, at]
 
     sib_copies = {}
-    loads[2].wait()
     loads[3].wait()
+    loads[4].wait()
     arrived[0, 1].wait_recv()
     multiply((0,))
     for r in range(NC):
@@ -217,53 +216,56 @@
         packed = jnp.where(lane == sub + k * TOK, value, packed)
     zbuf[0:1] = jnp.sum(packed, axis=0, keepdims=True)
 
-    @pl.when(c == 1)
-    def _():
-        pl.semaphore_wait(barrier, NC * ((NZ - 1) + (NX - 1) * NY))
-        pl.semaphore_signal(far, inc=1, device_id=core(0, 0), device_id_type=MESH)
-
-    @pl.when(c == 0)
+    @pl.when(clerk)
+    def _():
+        pl.semaphore_wait(barrier, NY * NC * (NZ - 1 + NX - 1))
+        for k, r in ((2, 0), (2, 1), (1, 0), (1, 1), (3, 0), (3, 1), (0, 1)):
+            pl.semaphore_signal(far, inc=1, device_id=device(k, r), device_id_type=MESH)
+
+    @pl.when(jnp.logical_not(clerk))
     def _():
         pl.semaphore_wait(far, 1)
 
     for dz in sorted(range(1, NZ), key=lambda d: -min(d, NZ - d)):
         remote(zbuf.at[0:1], zbuf.at[NZ - dz : NZ - dz + 1], z_sem.at[0], z_sem.at[1], device(0, 0, 0, dz)).start()
 
-    lg_copies = {}
-
-    def to_other_core(k):
-        mine = slot_of(k, 0)
-        lg_copies[k, 1] = start(remote(
-            logits.at[mine], logits.at[slot_of(k, 1)], lg_send.at[slot_of(k, 1)], lg_recv.at[slot_of(k, 1)], device(0, 1)
-        ))
-
-    for k in (1, 3, 2):
-        slot = slot_of(BACK[k], 0)
-        lg_copies[BACK[k], 0] = start(remote(
-            logits.at[0], logits.at[slot], lg_send.at[slot], lg_recv.at[slot], device(k, 0)
-        ))
-    to_other_core(0)
-
-    def exponents(slot, values):
-        for m in range(2):
-            top = jnp.max(values[m], axis=1, keepdims=True)
-            shifted[slot, m] = jnp.exp(values[m] - top)
-            tops[slot, m] = jnp.broadcast_to(top, (TOK, 128))
-
-    def arrive(k, r):
-        lg_copies[k, r].wait_recv()
+    def pass_logits(m, source, slot, target):
+        start(remote(logits.at[source, m], logits.at[slot, m], lg_send.at[slot, m], lg_recv.at[slot, m], target))
+
+    def arrive(m, k, r):
+        slot = slot_of(k, r)
+        landed = logits.at[slot, m]
+        pltpu.make_async_copy(landed, landed, lg_recv.at[slot, m]).wait()
         if r == 0:
-            to_other_core(k)
+            if (m, k) == (0, 3):
+                pass_logits(m, slot, slot_of(2, 0), device(1, 0))
+            if (m, k) == (1, 1):
+                pass_logits(m, slot, slot_of(2, 0), device(3, 0))
+            pass_logits(m, slot, slot_of(k, 1), device(0, 1))
+
+    def exponents(m, k, r):
         slot = slot_of(k, r)
-        exponents(slot, (logits[slot, 0], logits[slot, 1]))
+        values = logits[slot, m]
+        top = jnp.max(values, axis=1, keepdims=True)
+        shifted[slot, m] = jnp.exp(values - top)
+        tops[slot, m] = jnp.broadcast_to(top, (TOK, 128))
+
+    for m, k in ((0, 1), (1, 3), (1, 1), (0, 3)):
+        pass_logits(m, 0, slot_of(BACK[k], 0), device(k, 0))
+    for m in range(2):
+        pass_logits(m, 0, slot_of(0, 1), device(0, 1))
 
     shifted[0, 0] = exp_t
     shifted[0, 1] = exp_s
     tops[0, 0] = jnp.broadcast_to(top_t, (TOK, 128))
     tops[0, 1] = jnp.broadcast_to(top_s, (TOK, 128))
-    arrive(0, 1)
-    arrive(1, 0)
-    arrive(3, 0)
+    for m in range(2):
+        arrive(m, 0, 1)
+        exponents(m, 0, 1)
+    for m, k in ((0, 3), (1, 1), (1, 3), (0, 1)):
+        arrive(m, k, 0)
+    for m, k in ((0, 3), (1, 1), (1, 3), (0, 1)):
+        exponents(m, k, 0)
 
     pltpu.make_async_copy(zbuf.at[1:NZ], zbuf.at[1:NZ], z_sem.at[1]).wait()
     pbuf[0:1] = combine(zbuf[...].reshape(NZ, 1, 128))
@@ -272,10 +274,16 @@
         row = BACK[dx] * NY * NC + slot_of(BACK[k], r)
         remote(pbuf.at[0:1], pbuf.at[row : row + 1], p_sem.at[0], p_sem.at[1], device(k, r, dx)).start()
 
-    arrive(1, 1)
-    arrive(3, 1)
-    arrive(2, 0)
-    arrive(2, 1)
+    for m in range(2):
+        arrive(m, 2, 0)
+    for m, k in ((0, 3), (1, 1), (1, 3), (0, 1)):
+        arrive(m, k, 1)
+        exponents(m, k, 1)
+    for m in range(2):
+        exponents(m, 2, 0)
+    for m in range(2):
+        arrive(m, 2, 1)
+        exponents(m, 2, 1)
 
     everyone = pbuf.at[1 : NX * NY * NC]
     pltpu.make_async_copy(everyone, everyone, p_sem.at[1]).wait()
@@ -308,18 +316,9 @@
     pltpu.make_async_copy(everyone, everyone, p_sem.at[0]).wait()
 
 
-def final_kernel(pieces, cols_ref, grad_ref, loss_in, head_hbm, loss_ref, head, sem):
-    rows = head.shape[0] // pieces
-    copies = []
-    for i in range(pieces):
-        at = slice(i * rows, (i + 1) * rows)
-        head[at] = jnp.dot(cols_ref[at], grad_ref[...], preferred_element_type=F32).astype(BF16)
-        copy = pltpu.make_async_copy(head.at[at], head_hbm.at[at], sem.at[i])
-        copy.start()
-        copies.append(copy)
+def final_kernel(cols_ref, grad_ref, loss_in, head_ref, loss_ref):
+    head_ref[...] = jnp.dot(cols_ref[...], grad_ref[...], preferred_element_type=F32).astype(BF16)
     loss_ref[...] = loss_in[:, :TOK]
-    for copy in copies:
-        copy.wait()
 
 
 def on_device(teacher_batch, student_batch, positions, teacher_head, student_head):
@@ -328,21 +327,23 @@
     vocab = shard * NX * NZ
     wide = 128 * pl.cdiv(width_t + width_s, 128)
     groups = NY * NC
-    any_spec = pl.BlockSpec(memory_space=pl.ANY)
+    hbm = pl.BlockSpec(memory_space=pltpu.HBM)
+    in_hbm = functools.partial(pltpu.with_memory_space_constraint, memory_space=pltpu.HBM)
     vmem = pl.BlockSpec(memory_space=pltpu.VMEM)
     dma = pltpu.SemaphoreType.DMA
     grad, cols, loss = pl.pallas_call(
         functools.partial(exchange_kernel, vocab, width_t, width_s, shard),
         out_shape=(
-            jax.ShapeDtypeStruct((ROWS, shard), BF16),
-            jax.ShapeDtypeStruct((width_s, ROWS), BF16),
-            jax.ShapeDtypeStruct((1, 128), F32),
+            pltpu.VMEM((ROWS, shard), BF16),
+            pltpu.VMEM((width_s, ROWS), BF16),
+            pltpu.VMEM((1, 128), F32),
         ),
-        in_specs=[any_spec, any_spec, vmem, any_spec, any_spec],
+        in_specs=[hbm] * 5,
         out_specs=(vmem, vmem, vmem),
         scratch_shapes=[
             pltpu.VMEM(teacher_batch.shape, BF16),
             pltpu.VMEM(student_batch.shape, BF16),
+            pltpu.VMEM((1, TOK), jnp.int32),
             pltpu.VMEM(teacher_head.shape, BF16),
             pltpu.VMEM(student_head.shape, BF16),
             pltpu.VMEM((NY, NC, TOK, wide), BF16),
@@ -358,28 +359,29 @@
             pltpu.VMEM((groups, 2, TOK, 128), F32),
             pltpu.VMEM((NZ, 128), F32),
             pltpu.VMEM((NX * groups, 128), F32),
-            dma((4,)),
+            dma((5,)),
             dma((groups,)), dma((groups,)),
             dma((2, NY)), dma((2, NY)),
             dma((2,)), dma((2,)),
             dma((2, 2)), dma((2, 2)),
-            dma((groups,)), dma((groups,)),
+            dma((groups, 2)), dma((groups, 2)),
             dma((2,)), dma((2,)),
             pltpu.SemaphoreType.REGULAR,
             pltpu.SemaphoreType.REGULAR,
         ],
-        compiler_params=pltpu.CompilerParams(collective_id=0, has_side_effects=True),
-    )(teacher_batch, student_batch, positions.reshape(1, TOK), teacher_head, student_head)
-    pieces = 4
+        compiler_params=pltpu.CompilerParams(
+            collective_id=0, has_side_effects=True, vmem_limit_bytes=32 * 1024 * 1024
+        ),
+    )(*map(in_hbm, (teacher_batch, student_batch, positions.reshape(1, TOK), teacher_head, student_head)))
     head_grad, loss = pl.pallas_call(
-        functools.partial(final_kernel, pieces),
+        final_kernel,
         out_shape=(
             jax.ShapeDtypeStruct((width_s, shard), BF16),
             jax.ShapeDtypeStruct((1, TOK), F32),
         ),
         in_specs=[vmem] * 3,
-        out_specs=(any_spec, vmem),
-        scratch_shapes=[pltpu.VMEM((width_s, shard), BF16), dma((pieces,))],
+        out_specs=(vmem, vmem),
+        compiler_params=pltpu.CompilerParams(vmem_limit_bytes=16 * 1024 * 1024),
     )(cols, grad, loss)
     return head_grad, loss.reshape(TOK)
 

time: 48.1 us -> 45.1 us (0.938)
  Pallas kernels: 47.3 us -> 44.4 us
    pallas_call x1, Pallas kernels: 44.5 us -> 42.9 us  [on_device(): pl.pallas_call(functools.partial(exchange_kernel, vocab, width_t, width_s...]
    pallas_call x1, Pallas kernels: 2.78 us -> 1.45 us  [on_device(): pl.pallas_call(final_kernel, out_shape=(jax.ShapeDtypeStruct((width_s, sh...]
where the time goes in v3:
time: 45.1 us; the launch traced here: 45 us
  Pallas kernels  44.4 us (98%)
  between operations  0.64 us (1%)
    pallas_call x1, Pallas kernels, on_device(): pl.pallas_call(functools.partial(exchange_kernel, vocab, width_t, width_s...  42.9 us
    pallas_call x1, Pallas kernels, on_device(): pl.pallas_call(final_kernel, out_shape=(jax.ShapeDtypeStruct((width_s, sh...  1.45 us

profile of v3, /device:TPU:1, one launch (start us, length us, event | category | flops | bytes accessed | tf_op | source)
XLA Modules:
  0.0 45.0 jit_solution(7525161657319741158)
XLA Ops:
  0.6 42.9 %shard_map.68 = (bf16[128,1280]{1,0:T(8,128)(2,1)S(1)}, bf16[448,128]{1,0:T(8,128)(2,1)S(1)}, f32[1,128]{1,0:T(1,128)S(1)}) custom-call(bf16[20,5120]{1,0:T(8,128)(2,1)} %tb_hbm.1, bf16[20,3584]{1,0:T(8,128)(2,1)} %sb_hbm.1, s32[1,16]{1,0:T(1,128)} %bitcast.2, bf16[640,1280]{1,0:T(8,128)(2,1)} %th_hbm.1, bf16[448,1280]{1,0:T(8,128)(2,1)} %sh_hbm.1), custom_call_target="tpu_custom_call" | custom-call | tf_op jit(solution)/shard_map/pallas_call | solution.py:334
  43.5 1.5 %shard_map.69 = (bf16[448,1280]{1,0:T(8,128)(2,1)}, f32[1,16]{1,0:T(1,128)}) custom-call(bf16[448,128]{1,0:T(8,128)(2,1)S(1)} %get-tuple-element.7.cols_ref, bf16[128,1280]{1,0:T(8,128)(2,1)S(1)} %get-tuple-element.8.grad_ref, f32[1,128]{1,0:T(1,128)S(1)} %get-tuple-element.9.loss_in), custom_call_target="tpu_custom_call" | custom-call | tf_op jit(solution)/shard_map/pallas_call | solution.py:376

commit v4 on v3

--- a/solution.py
+++ b/solution.py
@@ -162,10 +162,6 @@
     for r in range(NC):
         arrived[2, r].wait_recv()
     multiply((2,))
-    for k in (1, 3):
-        for r in range(NC):
-            arrived[k, r].wait_recv()
-    multiply((1, 3))
 
     opp_copies = []
     for m, k in ((0, 1), (1, 3)):
@@ -173,6 +169,10 @@
         opp_copies.append(start(remote(
             chip.at[m, PLACE[2]], opp.at[m], opp_send.at[m], opp_recv.at[m], device(k, 0)
         )))
+    for k in (1, 3):
+        for r in range(NC):
+            arrived[k, r].wait_recv()
+    multiply((1, 3))
     ring_copies = {}
     for m, k in ((1, 1), (0, 3)):
         add_cores(m, k)
@@ -187,6 +187,12 @@
         ring_copies[m, k] = start(remote(
             merged.at[m], ring.at[m, k // 2], ring_send.at[m, k // 2], ring_recv.at[m, k // 2], device(k, 0)
         ))
+    @pl.when(clerk)
+    def _():
+        pl.semaphore_wait(barrier, NY * NC * (NZ - 1 + NX - 1))
+        for k, r in ((2, 0), (2, 1), (1, 0), (1, 1), (3, 0), (3, 1), (0, 1)):
+            pl.semaphore_signal(far, inc=1, device_id=device(k, r), device_id_type=MESH)
+
     add_cores(0, 0)
     add_cores(1, 0)
     cols_ref[...] = jnp.transpose(states[:, width_t : width_t + width_s].astype(F32)).astype(BF16)
@@ -215,12 +221,6 @@
     for k, value in enumerate(columns):
         packed = jnp.where(lane == sub + k * TOK, value, packed)
     zbuf[0:1] = jnp.sum(packed, axis=0, keepdims=True)
-
-    @pl.when(clerk)
-    def _():
-        pl.semaphore_wait(barrier, NY * NC * (NZ - 1 + NX - 1))
-        for k, r in ((2, 0), (2, 1), (1, 0), (1, 1), (3, 0), (3, 1), (0, 1)):
-            pl.semaphore_signal(far, inc=1, device_id=device(k, r), device_id_type=MESH)
 
     @pl.when(jnp.logical_not(clerk))
     def _():

time: 45.1 us -> 43.6 us (0.967)
  Pallas kernels: 44.4 us -> 42.8 us
    pallas_call x1, Pallas kernels: 42.9 us -> 41.4 us  [on_device(): pl.pallas_call(functools.partial(exchange_kernel, vocab, width_t, width_s...]
where the time goes in v4:
time: 43.6 us; the launch traced here: 43.5 us
  Pallas kernels  42.8 us (98%)
  between operations  0.64 us (1%)
    pallas_call x1, Pallas kernels, on_device(): pl.pallas_call(functools.partial(exchange_kernel, vocab, width_t, width_s...  41.4 us
    pallas_call x1, Pallas kernels, on_device(): pl.pallas_call(final_kernel, out_shape=(jax.ShapeDtypeStruct((width_s, sh...  1.45 us

profile of v4, /device:TPU:1, one launch (start us, length us, event | category | flops | bytes accessed | tf_op | source)
XLA Modules:
  0.0 43.5 jit_solution(6676291229067110811)
XLA Ops:
  0.6 41.4 %shard_map.68 = (bf16[128,1280]{1,0:T(8,128)(2,1)S(1)}, bf16[448,128]{1,0:T(8,128)(2,1)S(1)}, f32[1,128]{1,0:T(1,128)S(1)}) custom-call(bf16[20,5120]{1,0:T(8,128)(2,1)} %tb_hbm.1, bf16[20,3584]{1,0:T(8,128)(2,1)} %sb_hbm.1, s32[1,16]{1,0:T(1,128)} %bitcast.2, bf16[640,1280]{1,0:T(8,128)(2,1)} %th_hbm.1, bf16[448,1280]{1,0:T(8,128)(2,1)} %sh_hbm.1), custom_call_target="tpu_custom_call" | custom-call | tf_op jit(solution)/shard_map/pallas_call | solution.py:334
  42.0 1.4 %shard_map.69 = (bf16[448,1280]{1,0:T(8,128)(2,1)}, f32[1,16]{1,0:T(1,128)}) custom-call(bf16[448,128]{1,0:T(8,128)(2,1)S(1)} %get-tuple-element.7.cols_ref, bf16[128,1280]{1,0:T(8,128)(2,1)S(1)} %get-tuple-element.8.grad_ref, f32[1,128]{1,0:T(1,128)S(1)} %get-tuple-element.9.loss_in), custom_call_target="tpu_custom_call" | custom-call | tf_op jit(solution)/shard_map/pallas_call | solution.py:376

commit v5 on v4

--- a/solution.py
+++ b/solution.py
@@ -61,9 +61,6 @@
         pltpu.make_async_copy(src, dst, load_sem.at[i])
         for i, (src, dst) in enumerate(((pos_hbm, pos), (tb_hbm, tb), (sb_hbm, sb), (th_hbm, th), (sh_hbm, sh)))
     ]
-    for load in loads[:3]:
-        load.start()
-
     barrier = pltpu.get_barrier_semaphore()
     clerk = tok == CLERK
     for k, r in ((2, 0), (2, 1), (1, 0), (1, 1), (3, 0), (3, 1), (0, 1)):
@@ -71,7 +68,7 @@
         def _():
             pl.semaphore_signal(barrier, inc=1, device_id=device(k, r), device_id_type=MESH)
 
-    for load in loads[3:]:
+    for load in loads:
         load.start()
 
     loads[0].wait()
@@ -293,8 +290,9 @@
     t_lse = lanes(rows, 4 * TOK) + jnp.log(sum_t)
     s_lse = lanes(rows, 7 * TOK) + jnp.log(lanes(rows, 3 * TOK))
     entropy = t_lse - lanes(rows, TOK) / sum_t
-    weight = jnp.exp(-2.0 * entropy / math.log(vocab))
-    loss_ref[...] = (weight * (s_lse - lanes(rows, 2 * TOK) / sum_t - entropy))[0:1]
+    log_weight = entropy * (-2.0 / math.log(vocab))
+    loss_ref[...] = (jnp.exp(log_weight) * (s_lse - lanes(rows, 2 * TOK) / sum_t - entropy))[0:1]
+    log_scale = log_weight + math.log(vocab / TOK)
 
     lane = lax.broadcasted_iota(jnp.int32, (NY * NC, TOK, 128), 2)
     sub = lax.broadcasted_iota(jnp.int32, (NY * NC, TOK, 128), 1)
@@ -303,12 +301,13 @@
         spread = jnp.broadcast_to(values[:, None, :], (NY * NC, TOK, 128))
         return jnp.sum(jnp.where(lane == sub, spread, 0.0), axis=2, keepdims=True)
 
-    scale = column_of(vocab / TOK * weight)
-    scale_t = scale * jnp.exp(tops[:, 0] - column_of(t_lse))
-    scale_s = scale * jnp.exp(tops[:, 1] - column_of(s_lse))
+    scale_t = jnp.exp(tops[:, 0] + column_of(log_scale - t_lse))
+    scale_s = jnp.exp(tops[:, 1] + column_of(log_scale - s_lse))
     for slot in range(NY * NC):
-        grad = scale_s[slot, :, 0:1] * shifted[slot, 1] - scale_t[slot, :, 0:1] * shifted[slot, 0]
-        grad_ref[slot * TOK : (slot + 1) * TOK] = grad.astype(BF16)
+        for at in range(0, shard, 128):
+            cut = slice(at, at + 128)
+            grad = scale_s[slot] * shifted[slot, 1, :, cut] - scale_t[slot] * shifted[slot, 0, :, cut]
+            grad_ref[slot * TOK : (slot + 1) * TOK, cut] = grad.astype(BF16)
 
     for copy in sent:
         copy.wait_send()
@@ -316,9 +315,18 @@
     pltpu.make_async_copy(everyone, everyone, p_sem.at[0]).wait()
 
 
-def final_kernel(cols_ref, grad_ref, loss_in, head_ref, loss_ref):
-    head_ref[...] = jnp.dot(cols_ref[...], grad_ref[...], preferred_element_type=F32).astype(BF16)
-    loss_ref[...] = loss_in[:, :TOK]
+def final_kernel(pieces, cols_ref, grad_ref, loss_in, head_hbm, loss_hbm, head, loss, sem):
+    loss[...] = loss_in[:, :TOK]
+    copies = [pltpu.make_async_copy(loss, loss_hbm, sem.at[pieces])]
+    copies[0].start()
+    tall = head.shape[0] // pieces
+    for i in range(pieces):
+        at = slice(i * tall, (i + 1) * tall)
+        head[at] = jnp.dot(cols_ref[at], grad_ref[...], preferred_element_type=F32).astype(BF16)
+        copies.append(pltpu.make_async_copy(head.at[at], head_hbm.at[at], sem.at[i]))
+        copies[-1].start()
+    for copy in copies:
+        copy.wait()
 
 
 def on_device(teacher_batch, student_batch, positions, teacher_head, student_head):
@@ -373,14 +381,16 @@
             collective_id=0, has_side_effects=True, vmem_limit_bytes=32 * 1024 * 1024
         ),
     )(*map(in_hbm, (teacher_batch, student_batch, positions.reshape(1, TOK), teacher_head, student_head)))
+    pieces = 4
     head_grad, loss = pl.pallas_call(
-        final_kernel,
+        functools.partial(final_kernel, pieces),
         out_shape=(
             jax.ShapeDtypeStruct((width_s, shard), BF16),
             jax.ShapeDtypeStruct((1, TOK), F32),
         ),
         in_specs=[vmem] * 3,
-        out_specs=(vmem, vmem),
+        out_specs=(hbm, hbm),
+        scratch_shapes=[pltpu.VMEM((width_s, shard), BF16), pltpu.VMEM((1, TOK), F32), dma((pieces + 1,))],
         compiler_params=pltpu.CompilerParams(vmem_limit_bytes=16 * 1024 * 1024),
     )(cols, grad, loss)
     return head_grad, loss.reshape(TOK)

time: 43.6 us -> 43.4 us (level)
  no operation moved by 1% of the time
where the time goes in v5:
time: 43.4 us; the launch traced here: 43.3 us
  Pallas kernels  42.6 us (98%)
  between operations  0.64 us (1%)
    pallas_call x1, Pallas kernels, on_device(): pl.pallas_call(functools.partial(exchange_kernel, vocab, width_t, width_s...  41.3 us
    pallas_call x1, Pallas kernels, on_device(): pl.pallas_call(functools.partial(final_kernel, pieces), out_shape=(jax.Sh...  1.28 us

profile of v5, /device:TPU:1, one launch (start us, length us, event | category | flops | bytes accessed | tf_op | source)
XLA Modules:
  0.0 43.3 jit_solution(8852432575887080971)
XLA Ops:
  0.6 41.3 %shard_map.68 = (bf16[128,1280]{1,0:T(8,128)(2,1)S(1)}, bf16[448,128]{1,0:T(8,128)(2,1)S(1)}, f32[1,128]{1,0:T(1,128)S(1)}) custom-call(bf16[20,5120]{1,0:T(8,128)(2,1)} %tb_hbm.1, bf16[20,3584]{1,0:T(8,128)(2,1)} %sb_hbm.1, s32[1,16]{1,0:T(1,128)} %bitcast.2, bf16[640,1280]{1,0:T(8,128)(2,1)} %th_hbm.1, bf16[448,1280]{1,0:T(8,128)(2,1)} %sh_hbm.1), custom_call_target="tpu_custom_call" | custom-call | tf_op jit(solution)/shard_map/pallas_call | solution.py:342
  42.0 1.3 %shard_map.69 = (bf16[448,1280]{1,0:T(8,128)(2,1)}, f32[1,16]{1,0:T(1,128)}) custom-call(bf16[448,128]{1,0:T(8,128)(2,1)S(1)} %get-tuple-element.7.cols_ref, bf16[128,1280]{1,0:T(8,128)(2,1)S(1)} %get-tuple-element.8.grad_ref, f32[1,128]{1,0:T(1,128)S(1)} %get-tuple-element.9.loss_in), custom_call_target="tpu_custom_call" | custom-call | tf_op jit(solution)/shard_map/pallas_call | solution.py:385

commit v6 on v5

--- a/solution.py
+++ b/solution.py
@@ -282,7 +282,11 @@
         arrive(m, 2, 1)
         exponents(m, 2, 1)
 
+    for copy in sent:
+        copy.wait_send()
     everyone = pbuf.at[1 : NX * NY * NC]
+    pltpu.make_async_copy(zbuf.at[1:NZ], zbuf.at[1:NZ], z_sem.at[0]).wait()
+    pltpu.make_async_copy(everyone, everyone, p_sem.at[0]).wait()
     pltpu.make_async_copy(everyone, everyone, p_sem.at[1]).wait()
     rows = combine(pbuf[...].reshape(NX, NY * NC, 128))
 
@@ -308,11 +312,6 @@
             cut = slice(at, at + 128)
             grad = scale_s[slot] * shifted[slot, 1, :, cut] - scale_t[slot] * shifted[slot, 0, :, cut]
             grad_ref[slot * TOK : (slot + 1) * TOK, cut] = grad.astype(BF16)
-
-    for copy in sent:
-        copy.wait_send()
-    pltpu.make_async_copy(zbuf.at[1:NZ], zbuf.at[1:NZ], z_sem.at[0]).wait()
-    pltpu.make_async_copy(everyone, everyone, p_sem.at[0]).wait()
 
 
 def final_kernel(pieces, cols_ref, grad_ref, loss_in, head_hbm, loss_hbm, head, loss, sem):

time: 43.4 us -> 43.3 us (level)
  no operation moved by 1% of the time
where the time goes in v6:
time: 43.3 us; the launch traced here: 43.2 us
  Pallas kernels  42.6 us (98%)
  between operations  0.64 us (1%)
    pallas_call x1, Pallas kernels, on_device(): pl.pallas_call(functools.partial(exchange_kernel, vocab, width_t, width_s...  41.3 us
    pallas_call x1, Pallas kernels, on_device(): pl.pallas_call(functools.partial(final_kernel, pieces), out_shape=(jax.Sh...  1.28 us

profile of v6, /device:TPU:1, one launch (start us, length us, event | category | flops | bytes accessed | tf_op | source)
XLA Modules:
  0.0 43.2 jit_solution(14527609607765845689)
XLA Ops:
  0.6 41.3 %shard_map.68 = (bf16[128,1280]{1,0:T(8,128)(2,1)S(1)}, bf16[448,128]{1,0:T(8,128)(2,1)S(1)}, f32[1,128]{1,0:T(1,128)S(1)}) custom-call(bf16[20,5120]{1,0:T(8,128)(2,1)} %tb_hbm.1, bf16[20,3584]{1,0:T(8,128)(2,1)} %sb_hbm.1, s32[1,16]{1,0:T(1,128)} %bitcast.2, bf16[640,1280]{1,0:T(8,128)(2,1)} %th_hbm.1, bf16[448,1280]{1,0:T(8,128)(2,1)} %sh_hbm.1), custom_call_target="tpu_custom_call" | custom-call | tf_op jit(solution)/shard_map/pallas_call | solution.py:341
  41.9 1.3 %shard_map.69 = (bf16[448,1280]{1,0:T(8,128)(2,1)}, f32[1,16]{1,0:T(1,128)}) custom-call(bf16[448,128]{1,0:T(8,128)(2,1)S(1)} %get-tuple-element.7.cols_ref, bf16[128,1280]{1,0:T(8,128)(2,1)S(1)} %get-tuple-element.8.grad_ref, f32[1,128]{1,0:T(1,128)S(1)} %get-tuple-element.9.loss_in), custom_call_target="tpu_custom_call" | custom-call | tf_op jit(solution)/shard_map/pallas_call | solution.py:384

commit v7 on v6

--- a/solution.py
+++ b/solution.py
@@ -178,18 +178,18 @@
         ))
     for m, k in ((0, 1), (1, 3)):
         add_cores(m, k)
+    @pl.when(clerk)
+    def _():
+        pl.semaphore_wait(barrier, NY * NC * (NZ - 1 + NX - 1))
+        for k, r in ((2, 0), (2, 1), (1, 0), (1, 1), (3, 0), (3, 1), (0, 1)):
+            pl.semaphore_signal(far, inc=1, device_id=device(k, r), device_id_type=MESH)
+
     for m, k in ((0, 1), (1, 3)):
         opp_copies[m].wait_recv()
         merged[m] = chip[m, PLACE[k]] + opp[m]
         ring_copies[m, k] = start(remote(
             merged.at[m], ring.at[m, k // 2], ring_send.at[m, k // 2], ring_recv.at[m, k // 2], device(k, 0)
         ))
-    @pl.when(clerk)
-    def _():
-        pl.semaphore_wait(barrier, NY * NC * (NZ - 1 + NX - 1))
-        for k, r in ((2, 0), (2, 1), (1, 0), (1, 1), (3, 0), (3, 1), (0, 1)):
-            pl.semaphore_signal(far, inc=1, device_id=device(k, r), device_id_type=MESH)
-
     add_cores(0, 0)
     add_cores(1, 0)
     cols_ref[...] = jnp.transpose(states[:, width_t : width_t + width_s].astype(F32)).astype(BF16)

time: 43.3 us -> 43.3 us (level)
  no operation moved by 1% of the time
where the time goes in v7:
time: 43.3 us; the launch traced here: 43.2 us
  Pallas kernels  42.6 us (98%)
  between operations  0.64 us (1%)
    pallas_call x1, Pallas kernels, on_device(): pl.pallas_call(functools.partial(exchange_kernel, vocab, width_t, width_s...  41.3 us
    pallas_call x1, Pallas kernels, on_device(): pl.pallas_call(functools.partial(final_kernel, pieces), out_shape=(jax.Sh...  1.28 us

profile of v7, /device:TPU:1, one launch (start us, length us, event | category | flops | bytes accessed | tf_op | source)
XLA Modules:
  0.0 43.2 jit_solution(5092911729834086872)
XLA Ops:
  0.6 41.3 %shard_map.68 = (bf16[128,1280]{1,0:T(8,128)(2,1)S(1)}, bf16[448,128]{1,0:T(8,128)(2,1)S(1)}, f32[1,128]{1,0:T(1,128)S(1)}) custom-call(bf16[20,5120]{1,0:T(8,128)(2,1)} %tb_hbm.1, bf16[20,3584]{1,0:T(8,128)(2,1)} %sb_hbm.1, s32[1,16]{1,0:T(1,128)} %bitcast.2, bf16[640,1280]{1,0:T(8,128)(2,1)} %th_hbm.1, bf16[448,1280]{1,0:T(8,128)(2,1)} %sh_hbm.1), custom_call_target="tpu_custom_call" | custom-call | tf_op jit(solution)/shard_map/pallas_call | solution.py:341
  41.9 1.3 %shard_map.69 = (bf16[448,1280]{1,0:T(8,128)(2,1)}, f32[1,16]{1,0:T(1,128)}) custom-call(bf16[448,128]{1,0:T(8,128)(2,1)S(1)} %get-tuple-element.7.cols_ref, bf16[128,1280]{1,0:T(8,128)(2,1)S(1)} %get-tuple-element.8.grad_ref, f32[1,128]{1,0:T(1,128)S(1)} %get-tuple-element.9.loss_in), custom_call_target="tpu_custom_call" | custom-call | tf_op jit(solution)/shard_map/pallas_call | solution.py:384

commit v8 on v7

--- a/solution.py
+++ b/solution.py
@@ -18,6 +18,12 @@
 ROWS = NY * PAIR
 PLACE = {0: 0, 1: 1, 3: 2, 2: 3}
 BACK = {0: 0, 1: 3, 2: 2, 3: 1}
+
+
+FAR_FIRST = sorted(
+    [(0, dz) for dz in range(1, NZ)] + [(dx, 0) for dx in range(1, NX)],
+    key=lambda step: -min(step[0], NX - step[0]) - min(step[1], NZ - step[1]),
+)
 
 
 def slot_of(k, r):
@@ -125,7 +131,7 @@
                 ))
     states[:TOK] = picked[0, c]
 
-    for dx, dz in [(0, dz) for dz in range(1, NZ)] + [(dx, 0) for dx in range(1, NX)]:
+    for dx, dz in FAR_FIRST:
         there = (CLERK, device(0, 0, dx, dz)[1])
         pl.semaphore_signal(barrier, inc=1, device_id=there, device_id_type=MESH)
 

time: 43.3 us -> 43.3 us (level)
  no operation moved by 1% of the time
where the time goes in v8:
time: 43.3 us; the launch traced here: 43.2 us
  Pallas kernels  42.6 us (98%)
  between operations  0.64 us (1%)
    pallas_call x1, Pallas kernels, on_device(): pl.pallas_call(functools.partial(exchange_kernel, vocab, width_t, width_s...  41.3 us
    pallas_call x1, Pallas kernels, on_device(): pl.pallas_call(functools.partial(final_kernel, pieces), out_shape=(jax.Sh...  1.28 us

profile of v8, /device:TPU:1, one launch (start us, length us, event | category | flops | bytes accessed | tf_op | source)
XLA Modules:
  0.0 43.2 jit_solution(3888955203512564360)
XLA Ops:
  0.6 41.3 %shard_map.68 = (bf16[128,1280]{1,0:T(8,128)(2,1)S(1)}, bf16[448,128]{1,0:T(8,128)(2,1)S(1)}, f32[1,128]{1,0:T(1,128)S(1)}) custom-call(bf16[20,5120]{1,0:T(8,128)(2,1)} %tb_hbm.1, bf16[20,3584]{1,0:T(8,128)(2,1)} %sb_hbm.1, s32[1,16]{1,0:T(1,128)} %bitcast.2, bf16[640,1280]{1,0:T(8,128)(2,1)} %th_hbm.1, bf16[448,1280]{1,0:T(8,128)(2,1)} %sh_hbm.1), custom_call_target="tpu_custom_call" | custom-call | tf_op jit(solution)/shard_map/pallas_call | solution.py:347
  41.9 1.3 %shard_map.69 = (bf16[448,1280]{1,0:T(8,128)(2,1)}, f32[1,16]{1,0:T(1,128)}) custom-call(bf16[448,128]{1,0:T(8,128)(2,1)S(1)} %get-tuple-element.7.cols_ref, bf16[128,1280]{1,0:T(8,128)(2,1)S(1)} %get-tuple-element.8.grad_ref, f32[1,128]{1,0:T(1,128)S(1)} %get-tuple-element.9.loss_in), custom_call_target="tpu_custom_call" | custom-call | tf_op jit(solution)/shard_map/pallas_call | solution.py:390
